TPU v7x, 256 devices: a whole 4x4x8 slice. The times are simulated.
256 devices in a mesh: wide: 32 (over x_lo, z, core), narrow: 8 (over x_hi, y).
Axes of the slice: x: 4 (x_hi: 2, x_lo: 2; x = x_hi * 2 + x_lo), y: 4, z: 8, core: 2. Of those that a mesh axis runs over, the one named last changes fastest.
Arguments:
- activations: float32 [1024, 17408], P('wide', 'narrow'), may hold values from -6 to 6
- act_basis: float32 [17408, 17408], P('narrow', 'wide'), may hold values from -0.046875 to 0.046875
- grads: float32 [1024, 5120], P(None, 'wide'), may hold values from -0.3 to 0.3
- grad_basis: float32 [5120, 5120], P('wide', 'narrow'), may hold values from -0.078125 to 0.078125
- seq_ids: int32 [1024], replicated, may hold values from 0 to 3, never falling along the last dimension, each value on 1 to 512 neighbouring positions
Outputs:
- eigenvalues: float32 [17408, 5120], P('wide', 'narrow')
Inputs may be any that keep to these rules, and one draw needn't show every extreme that they name: `seq_ids`: never falling along the rows; every sequence has at least one row and at most 512 rows, and one sequence has exactly 512.
All inputs are finite; a program needn't handle non-finite values.
Results may differ from a plain program's by a relative error of at most 0.0003.
Values sent between devices are 32-bit elements; how exact they have to be, the bound alone decides.
No kernel may reach another device: no remote copies, remote signals or barrier semaphores. Data moves between devices by JAX's collectives and lax.ppermute only.
A program may use at most 64 MiB of HBM per device.

v0:
```python
import jax
import jax.numpy as jnp
from jax import lax
from jax.sharding import Mesh
from jax.sharding import PartitionSpec as P

SEQS = 4
SEQ_MOST = 512
WIDE = ("wide_0", "wide_1", "wide_2")


def filled_up(lines, devices):
    spare = -len(lines) % devices
    return jnp.pad(lines, [(0, spare)] + [(0, 0)] * (lines.ndim - 1))


def from_everyone(value, axis):
    devices = lax.axis_size(axis)
    return lax.all_to_all(
        jnp.broadcast_to(value[None], (devices, *value.shape)), axis, 0, 0, tiled=True
    )


def in_order(blocks, dim):
    blocks = jnp.moveaxis(blocks, 0, dim)
    dims = blocks.shape
    return blocks.reshape(*dims[:dim], dims[dim] * dims[dim + 1], *dims[dim + 2 :])


def gather_axes(value, axes, dim):
    far, near = axes
    first = from_everyone(value, far)
    blocks = jnp.swapaxes(from_everyone(first, near), 0, 1)
    return in_order(blocks.reshape(-1, *value.shape), dim)


def in_blocks(value, dim, devices):
    dims = value.shape
    blocks = value.reshape(*dims[:dim], devices, dims[dim] // devices, *dims[dim + 1 :])
    return jnp.moveaxis(blocks, dim, 0)


def sent_and_summed(value, axis, dim):
    blocks = in_blocks(value, dim, lax.axis_size(axis))
    arrived = lax.all_to_all(blocks, axis, split_axis=0, concat_axis=0, tiled=True)
    return arrived.sum(axis=0)


def summed_rows(value, axes, dim):
    far, near = axes
    blocks = in_blocks(value, dim, lax.axis_size(far))
    nearer = sent_and_summed(blocks, near, dim + 1)
    arrived = lax.all_to_all(nearer, far, split_axis=0, concat_axis=0, tiled=True)
    return arrived.sum(axis=0)


def nested_sum(value, axes):
    lines = value.reshape(-1, value.shape[-1])
    padded = filled_up(lines, lax.axis_size(axes[0]) * lax.axis_size(axes[1]))
    whole = gather_axes(summed_rows(padded, axes, 0), axes, 0)
    return lax.slice_in_dim(whole, 0, len(lines)).reshape(value.shape)


def seq_window(rotated_acts, rotated_grads, seq_ids, seq_label):
    token_rows = rotated_grads.shape[0]
    first_row = jnp.sum((seq_ids < seq_label).astype(jnp.int32))
    window_start = jnp.minimum(first_row, token_rows - SEQ_MOST)
    acts_window = lax.dynamic_slice_in_dim(rotated_acts, window_start, SEQ_MOST, 0)
    grads_window = lax.dynamic_slice_in_dim(rotated_grads, window_start, SEQ_MOST, 0)
    ids_window = lax.dynamic_slice_in_dim(seq_ids, window_start, SEQ_MOST, 0)
    seq_mask = (ids_window == seq_label).astype(jnp.float32)[:, None]
    return (acts_window, grads_window * seq_mask)


def per_device(activations, act_basis, grads, grad_basis, seq_ids):
    highest = lax.Precision.HIGHEST
    gathered = lax.all_gather(activations, WIDE, axis=0, tiled=True)
    partial_acts = jnp.dot(
        gathered, act_basis, precision=highest, preferred_element_type=jnp.float32
    )
    rotated_acts = lax.psum(partial_acts, "narrow")
    partial_grads = jnp.dot(
        grads, grad_basis, precision=highest, preferred_element_type=jnp.float32
    )
    rotated_grads = nested_sum(partial_grads, (("wide_0", "wide_1"), "wide_2"))
    out_cols = rotated_grads.shape[1]
    running = jnp.zeros((rotated_acts.shape[1], out_cols), jnp.float32)
    for seq_label in range(SEQS):
        acts_window, grads_window = seq_window(rotated_acts, rotated_grads, seq_ids, seq_label)
        moment = jnp.dot(
            acts_window.T, grads_window, precision=highest, preferred_element_type=jnp.float32
        )
        running = running + moment * moment
    return running / jnp.float32(SEQS)


def solution(mesh):
    split = Mesh(
        mesh.devices.reshape(2, 8, 2, mesh.shape["narrow"]),
        ("wide_0", "wide_1", "wide_2", "narrow"),
    )
    return jax.shard_map(
        per_device,
        mesh=split,
        in_specs=(P(WIDE, "narrow"), P("narrow", WIDE), P(None, WIDE), P(WIDE, "narrow"), P()),
        out_specs=P(WIDE, "narrow"),
        check_vma=False,
    )
```

profile of v0, /device:TPU:32, one launch (start us, length us, event | category | flops | bytes accessed | tf_op | source)
XLA Modules:
  0.0 276.0 jit_solution(7294936986308628746)
XLA Ops:
  6.5 0.0 copy-start
  6.5 0.0 all-gather.2.cloned.1.call-start
  6.5 0.7 all-gather.2.cloned.1.call-update
  7.3 0.4 copy-done
  7.6 3.9 %fusion.29 = f32[1024,640]{1,0:T(8,128)S(1)} fusion(f32[1024,160]{0,1:T(8,128)S(1)} %copy-done, f32[160,640]{1,0:T(8,128)} %param.8), kind=kOutput, calls=%fused_computation.42 | convolution fusion | flops 1258291200 | bytes 3686400 | tf_op jit(solution)/shard_map/dot_general | solution.py:82
  11.6 0.2 copy.11
  11.8 5.8 %all_to_all.20 = f32[2,16,32,640]{3,2,1,0:T(8,128)S(1)} all-to-all(f32[2,16,32,640]{3,2,1,0:T(8,128)S(1)} %bitcast.15), channel_id=1, replica_groups=mesh['wide_0'=2,'wide_1'=8,'wide_2'=2,'narrow'=8] {'wide_2'}, dimensions={0} | all-to-all | bytes 5242880 | tf_op jit(solution)/shard_map/all_to_all | solution.py:45
  17.6 1.3 reduce_sum.55
  18.9 54.5 %all_to_all.21 = f32[16,32,640]{2,1,0:T(8,128)S(1)} all-to-all(f32[16,32,640]{2,1,0:T(8,128)} %reduce_sum.55), channel_id=1, replica_groups=mesh['wide_0'=2,'wide_1'=8,'wide_2'=2,'narrow'=8] {'wide_0','wide_1'}, dimensions={0} | all-to-all | bytes 2621440 | tf_op jit(solution)/shard_map/all_to_all | solution.py:53
  73.5 0.1 reduce_sum.56
  73.5 1.2 broadcast_in_dim.4
  74.7 6.4 %all-to-all-start.2 = ((f32[16,32,640]{2,1,0:T(8,128)}), f32[16,32,640]{2,1,0:T(8,128)S(1)}, u32[]{:S(2)}, u32[]{:S(2)}) async-start(f32[16,32,640]{2,1,0:T(8,128)} %broadcast_in_dim.4), calls=%async_computation.2 | async-start | bytes 2621440 | tf_op jit(solution)/shard_map/all_to_all | solution.py:19
  81.2 0.0 all-reduce.2.cloned.1.call-start
  81.2 52.6 %all-gather.2.cloned.1.call-done = f32[1024,2176]{1,0:T(8,128)} async-done(((f32[32,2176]{1,0:T(8,128)}), f32[1024,2176]{1,0:T(8,128)}) %all-gather.2.cloned.1.call-update) | async-done | bytes 8912912 | tf_op jit(solution)/shard_map/all_gather | solution.py:77
  133.8 21.9 %fusion.28 = f32[1024,544]{0,1:T(8,128)} fusion(f32[1024,2176]{1,0:T(8,128)} %all-gather.2.cloned.1.call-done, f32[2176,544]{0,1:T(8,128)} %param.6), kind=kOutput, calls=%fused_computation.41 | convolution fusion | flops 14545846272 | bytes 15876096 | tf_op jit(solution)/shard_map/dot_general | solution.py:78
  155.7 0.0 copy-start.2
  155.7 0.0 all-reduce.2.cloned.1.call-update
  155.7 0.7 copy-done.2
  156.4 0.7 convert_reduce_fusion
  159.8 0.1 fusion.27
  159.9 0.0 all-to-all-done.2
  159.9 0.3 broadcast_in_dim.5
  160.2 5.8 %all_to_all.22 = f32[2,16,32,640]{3,2,1,0:T(8,128)S(1)} all-to-all(f32[2,16,32,640]{3,2,1,0:T(8,128)S(1)} %broadcast_in_dim.5), channel_id=1, replica_groups=mesh['wide_0'=2,'wide_1'=8,'wide_2'=2,'narrow'=8] {'wide_2'}, dimensions={0} | all-to-all | bytes 5242880 | tf_op jit(solution)/shard_map/all_to_all | solution.py:19
  166.0 0.2 copy.9
  166.2 87.8 %all-reduce.2.cloned.1.call-done = f32[1024,544]{0,1:T(8,128)} async-done(((f32[1024,544]{0,1:T(8,128)}), f32[1024,544]{0,1:T(8,128)}) %all-reduce.2.cloned.1.call-update) | async-done | bytes 2228240 | tf_op jit(solution)/shard_map/psum | solution.py:81
  254.0 0.0 copy-start.1
  254.0 4.5 %convolution_multiply_fusion.1 = f32[544,640]{1,0:T(8,128)S(1)} fusion(f32[1024,640]{1,0:T(8,128)S(1)} %bitcast.11, s32[]{:T(128)S(6)} %select_n.10, f32[1024,544]{0,1:T(8,128)} %all-reduce.2.cloned.1.call-done, f32[512]{0:T(512)S(1)} %get-tuple-element.10), kind=kOutput, calls=%fused_computation.2 | convolution fusion | flops 2139770880 | bytes 3820544 | tf_op jit(solution)/shard_map/dot_general | solution.py:90
  258.5 0.0 copy-done.1
  258.5 3.1 %convolution_multiply_fusion.2 = f32[544,640]{1,0:T(8,128)S(1)} fusion(f32[1024,640]{1,0:T(8,128)S(1)} %bitcast.12, s32[]{:T(128)S(6)} %select_n.9, f32[1024,544]{0,1:T(8,128)S(1)} %copy-done.1, f32[512]{0:T(512)S(1)} %get-tuple-element.12), kind=kOutput, calls=%fused_computation.3 | convolution fusion | flops 2139770880 | bytes 3820544 | tf_op jit(solution)/shard_map/dot_general | solution.py:90
  261.7 3.2 %fusion.1 = f32[544,640]{1,0:T(8,128)S(1)} fusion(f32[544,640]{1,0:T(8,128)S(1)} %convolution_multiply_fusion.1, f32[544,640]{1,0:T(8,128)S(1)} %convolution_multiply_fusion.2, f32[1024,640]{1,0:T(8,128)S(1)} %bitcast.13, s32[]{:T(128)S(6)} %select_n.8, f32[1024,544]{0,1:T(8,128)S(1)} %copy-done.1, f32[512]{0:T(512)S(1)} %get-tuple-element.11), kind=kOutput, calls=%fused_computation.6 | convolution fusion | flops 2140467200 | bytes 6605824 | tf_op jit(solution)/shard_map/dot_general | solution.py:90
  264.9 4.2 %fusion.3 = f32[544,640]{1,0:T(8,128)} fusion(f32[544,640]{1,0:T(8,128)S(1)} %fusion.1, f32[1024,640]{1,0:T(8,128)S(1)} %bitcast.14, s32[]{:T(128)S(6)} %select_n.11, f32[1024,544]{0,1:T(8,128)S(1)} %copy-done.1, f32[512]{0:T(512)S(1)} %get-tuple-element.9), kind=kOutput, calls=%fused_computation.8 | convolution fusion | flops 2140467200 | bytes 5213184 | tf_op jit(solution)/shard_map/dot_general | solution.py:90
Async XLA Ops:
  6.5 1.1 copy-start
  6.5 127.2 %all-gather.2.cloned.1.call-start = ((), (), s32[]{:S(2)}) async-start(), calls=%async_computation.4 | async-start | bytes 9191424 | tf_op jit(solution)/shard_map/all_gather | solution.py:77
  74.7 85.1 %all-to-all-start.2 = ((f32[16,32,640]{2,1,0:T(8,128)}), f32[16,32,640]{2,1,0:T(8,128)S(1)}, u32[]{:S(2)}, u32[]{:S(2)}) async-start(f32[16,32,640]{2,1,0:T(8,128)} %broadcast_in_dim.4), calls=%async_computation.2 | async-start | bytes 2621440 | tf_op jit(solution)/shard_map/all_to_all | solution.py:19
  81.2 172.9 %all-reduce.2.cloned.1.call-start = ((), (), s32[]{:S(2)}) async-start(), calls=%async_computation.5 | async-start | bytes 4456448 | tf_op jit(solution)/shard_map/psum | solution.py:81
  155.7 0.7 copy-start.2
  254.0 4.5 %copy-start.1 = (f32[1024,544]{0,1:T(8,128)S(1)}, f32[1024,544]{0,1:T(8,128)}, u32[]{:S(2)}) copy-start(f32[1024,544]{0,1:T(8,128)} %all-reduce.2.cloned.1.call-done) | copy-start | bytes 6684676
Sparse Core Ops, SparseCore 0:
  9.2 124.5 all-gather.1
  155.9 98.0 all-reduce.1
where the time goes:
time: 276 us
  waiting for transfers between devices  141 us (51%)
  blocking collectives  66.2 us (24%)
  matrix products  41 us (15%)
  between operations  16.1 us (6%)
  starting transfers between devices  6.48 us (2%)
  local copies, waits for them, and re-layouts  2.9 us (1%)
    psum x1, waiting for transfers between devices, per_device(): rotated_acts = lax.psum(partial_acts, 'narrow')  87.8 us
    all_to_all x1, blocking collectives, summed_rows(): lax.all_to_all(nearer, far, split_axis=0, concat_axis=0, tiled=True)  54.5 us
    all_gather x1, waiting for transfers between devices, per_device(): gathered = lax.all_gather(activations, WIDE, axis=0, tiled=True)  52.6 us
    dot_general x1, matrix products, per_device(): jnp.dot(gathered, act_basis, precision=highest, preferred_element_type=jn...  21.9 us
    dot_general x4, matrix products, per_device(): jnp.dot(acts_window.T, grads_window, precision=highest, preferred_element...  15.1 us
    all_to_all x1, starting transfers between devices, from_everyone(): lax.all_to_all(jnp.broadcast_to(value[None], (devices, *value.shape)), ax...  6.44 us
    all_to_all x1, blocking collectives, from_everyone(): lax.all_to_all(jnp.broadcast_to(value[None], (devices, *value.shape)), ax...  5.84 us
    all_to_all x1, blocking collectives, sent_and_summed(): lax.all_to_all(blocks, axis, split_axis=0, concat_axis=0, tiled=True)  5.84 us
  transfers between devices with their start and end apart: 3, of which 2 were waited for; matrix products, arithmetic and copies ran while one was open for 11% of the time, Pallas kernels for 0%

commit v1 on v0

--- a/solution.py
+++ b/solution.py
@@ -78,7 +78,7 @@
     partial_acts = jnp.dot(
         gathered, act_basis, precision=highest, preferred_element_type=jnp.float32
     )
-    rotated_acts = lax.psum(partial_acts, "narrow")
+    rotated_acts = jnp.sum(lax.all_gather(partial_acts, "narrow"), axis=0)
     partial_grads = jnp.dot(
         grads, grad_basis, precision=highest, preferred_element_type=jnp.float32
     )

time: 276 us -> 365 us (1.32)
  waiting for transfers between devices: 141 us -> 224 us
  local copies, waits for them, and re-layouts: 2.9 us -> 22.3 us
  blocking collectives: 66.2 us -> 51.3 us
  other arithmetic: 2.23 us -> 6.96 us
    all_gather x0 -> x1, waiting for transfers between devices: none -> 118 us  [per_device(): rotated_acts = jnp.sum(lax.all_gather(partial_acts, 'narrow'), axis=0)]
    psum x1 -> x0, waiting for transfers between devices: 87.8 us -> none  [per_device(): rotated_acts = lax.psum(partial_acts, 'narrow')]
    all_to_all x1, waiting for transfers between devices: 0.01 us -> 28.7 us  [from_everyone(): lax.all_to_all(jnp.broadcast_to(value[None], (devices, *value.shape)), ax...]
    all_gather x1, waiting for transfers between devices: 52.6 us -> 76.9 us  [per_device(): gathered = lax.all_gather(activations, WIDE, axis=0, tiled=True)]
    unnamed x6 -> x9, local copies, waits for them, and re-layouts: 1.03 us -> 20.4 us
    all_to_all x1, blocking collectives: 54.5 us -> 39.6 us  [summed_rows(): lax.all_to_all(nearer, far, split_axis=0, concat_axis=0, tiled=True)]
    reduce_sum x0 -> x1, other arithmetic: none -> 4.74 us  [per_device(): rotated_acts = jnp.sum(lax.all_gather(partial_acts, 'narrow'), axis=0)]
  transfers between devices with their start and end apart: 3 -> 3, of which waited for: 2 -> 3; matrix products, arithmetic and copies ran while one was open for 11% -> 2% of each run, Pallas kernels for 0% -> 0%
where the time goes in v1:
time: 365 us; the launch traced here: 363 us
  waiting for transfers between devices  224 us (61%)
  blocking collectives  51.3 us (14%)
  matrix products  38.5 us (11%)
  local copies, waits for them, and re-layouts  22.3 us (6%)
  between operations  15.9 us (4%)
  other arithmetic  6.96 us (2%)
  starting transfers between devices  4.44 us (1%)
    all_gather x1, waiting for transfers between devices, per_device(): rotated_acts = jnp.sum(lax.all_gather(partial_acts, 'narrow'), axis=0)  118 us
    all_gather x1, waiting for transfers between devices, per_device(): gathered = lax.all_gather(activations, WIDE, axis=0, tiled=True)  76.9 us
    all_to_all x1, blocking collectives, summed_rows(): lax.all_to_all(nearer, far, split_axis=0, concat_axis=0, tiled=True)  39.6 us
    all_to_all x1, waiting for transfers between devices, from_everyone(): lax.all_to_all(jnp.broadcast_to(value[None], (devices, *value.shape)), ax...  28.7 us
    dot_general x1, matrix products, per_device(): jnp.dot(gathered, act_basis, precision=highest, preferred_element_type=jn...  21.9 us
    unnamed x9, local copies, waits for them, and re-layouts  20.4 us
    dot_general x4, matrix products, per_device(): jnp.dot(acts_window.T, grads_window, precision=highest, preferred_element...  13.7 us
  transfers between devices with their start and end apart: 3, of which 3 were waited for; matrix products, arithmetic and copies ran while one was open for 2% of the time, Pallas kernels for 0%

profile of v1, /device:TPU:32, one launch (start us, length us, event | category | flops | bytes accessed | tf_op | source)
XLA Modules:
  0.0 363.4 jit_solution(13672851331560349913)
XLA Ops:
  6.5 0.0 copy-start
  6.5 0.0 all-gather.4.cloned.1.call-start
  6.5 0.7 all-gather.4.cloned.1.call-update
  7.3 0.0 all-gather.6.cloned.1.call-start
  7.3 76.9 %all-gather.4.cloned.1.call-done = f32[1024,2176]{1,0:T(8,128)} async-done(((f32[32,2176]{1,0:T(8,128)}), f32[1024,2176]{1,0:T(8,128)}) %all-gather.4.cloned.1.call-update) | async-done | bytes 8912912 | tf_op jit(solution)/shard_map/all_gather | solution.py:77
  84.2 21.9 %fusion.28 = f32[1024,544]{0,1:T(8,128)} fusion(f32[1024,2176]{1,0:T(8,128)} %all-gather.4.cloned.1.call-done, f32[2176,544]{0,1:T(8,128)} %param.6), kind=kOutput, calls=%fused_computation.42 | convolution fusion | flops 14545846272 | bytes 15876096 | tf_op jit(solution)/shard_map/dot_general | solution.py:78
  106.0 0.0 copy-start.2
  106.0 0.0 all-gather.6.cloned.1.call-update
  106.1 0.0 copy-done
  106.1 1.0 copy-done.2
  107.0 2.9 fusion.29
  110.0 0.2 copy.12
  110.2 5.8 %all_to_all.20 = f32[2,16,32,640]{3,2,1,0:T(8,128)S(1)} all-to-all(f32[2,16,32,640]{3,2,1,0:T(8,128)S(1)} %bitcast.21), channel_id=1, replica_groups=mesh['wide_0'=2,'wide_1'=8,'wide_2'=2,'narrow'=8] {'wide_2'}, dimensions={0} | all-to-all | bytes 5242880 | tf_op jit(solution)/shard_map/all_to_all | solution.py:45
  116.0 1.3 reduce_sum.65
  117.4 39.6 %all_to_all.21 = f32[16,32,640]{2,1,0:T(8,128)S(1)} all-to-all(f32[16,32,640]{2,1,0:T(8,128)} %reduce_sum.65), channel_id=1, replica_groups=mesh['wide_0'=2,'wide_1'=8,'wide_2'=2,'narrow'=8] {'wide_0','wide_1'}, dimensions={0} | all-to-all | bytes 2621440 | tf_op jit(solution)/shard_map/all_to_all | solution.py:53
  157.0 0.1 reduce_sum.66
  157.0 1.2 broadcast_in_dim.4
  158.2 0.0 copy-start.3
  158.2 4.4 %all-to-all-start.2 = ((f32[16,32,640]{2,1,0:T(8,128)}), f32[16,32,640]{2,1,0:T(8,128)S(1)}, u32[]{:S(2)}, u32[]{:S(2)}) async-start(f32[16,32,640]{2,1,0:T(8,128)} %broadcast_in_dim.4), calls=%async_computation.2 | async-start | bytes 2621440 | tf_op jit(solution)/shard_map/all_to_all | solution.py:19
  162.6 0.0 copy-done.3
  162.6 0.7 convert_reduce_fusion
  165.8 0.1 fusion.27
  165.8 28.7 %all-to-all-done.2 = f32[16,32,640]{2,1,0:T(8,128)S(1)} async-done(((f32[16,32,640]{2,1,0:T(8,128)}), f32[16,32,640]{2,1,0:T(8,128)S(1)}, u32[]{:S(2)}, u32[]{:S(2)}) %all-to-all-start.2) | async-done | bytes 1310752 | tf_op jit(solution)/shard_map/all_to_all | solution.py:19
  194.5 0.3 broadcast_in_dim.5
  194.8 5.8 %all_to_all.22 = f32[2,16,32,640]{3,2,1,0:T(8,128)S(1)} all-to-all(f32[2,16,32,640]{3,2,1,0:T(8,128)S(1)} %broadcast_in_dim.5), channel_id=1, replica_groups=mesh['wide_0'=2,'wide_1'=8,'wide_2'=2,'narrow'=8] {'wide_2'}, dimensions={0} | all-to-all | bytes 5242880 | tf_op jit(solution)/shard_map/all_to_all | solution.py:19
  200.7 0.2 copy.9
  200.9 117.8 %all-gather.6.cloned.1.call-done = f32[8192,544]{0,1:T(8,128)} async-done(((f32[1024,544]{0,1:T(8,128)}), f32[8192,544]{0,1:T(8,128)}) %all-gather.6.cloned.1.call-update) | async-done | bytes 17825808 | tf_op jit(solution)/shard_map/all_gather | solution.py:81
  318.6 19.4 %copy.10 = f32[68,8,8,1024]{3,2,1,0:T(8,128)S(1)} copy(f32[68,8,8,1024]{3,1,2,0:T(8,128)} %bitcast.20) | data formatting | bytes 35651584
  338.1 4.7 %bitcast_reduce_fusion = f32[1024,544]{0,1:T(8,128)S(1)} fusion(f32[68,8,8,1024]{3,2,1,0:T(8,128)S(1)} %copy.10), kind=kLoop, calls=%fused_computation | loop fusion | flops 3899392 | bytes 20054016 | tf_op jit(solution)/shard_map/reduce_sum | solution.py:81
  342.8 3.1 convolution_multiply_fusion.1
  345.9 3.1 convolution_multiply_fusion.2
  349.1 3.2 fusion.1
  352.3 0.0 copy-start.1
  352.3 4.2 %fusion.3 = f32[544,640]{1,0:T(8,128)} fusion(f32[544,640]{1,0:T(8,128)S(1)} %fusion.1, f32[1024,640]{1,0:T(8,128)S(1)} %bitcast.19, s32[]{:T(128)S(6)} %select_n.11, f32[1024,544]{0,1:T(8,128)S(1)} %bitcast_reduce_fusion, f32[512]{0:T(512)S(1)} %get-tuple-element.9), kind=kOutput, calls=%fused_computation.9 | convolution fusion | flops 2140467200 | bytes 5213184 | tf_op jit(solution)/shard_map/dot_general | solution.py:90
  356.6 0.0 copy-done.1
Async XLA Ops:
  6.5 99.5 %copy-start = (f32[1024,160]{0,1:T(8,128)S(1)}, f32[1024,160]{0,1:T(8,128)}, u32[]{:S(2)}) copy-start(f32[1024,160]{0,1:T(8,128)} %param.7) | copy-start | bytes 1966084
  6.5 77.6 %all-gather.4.cloned.1.call-start = ((), (), s32[]{:S(2)}) async-start(), calls=%async_computation.4 | async-start | bytes 9191424 | tf_op jit(solution)/shard_map/all_gather | solution.py:77
  7.3 311.4 %all-gather.6.cloned.1.call-start = ((), (), s32[]{:S(2)}) async-start(), calls=%async_computation.5 | async-start | bytes 20054016 | tf_op jit(solution)/shard_map/all_gather | solution.py:81
  106.0 1.0 copy-start.2
  158.2 4.4 %copy-start.3 = (s32[1024]{0:T(1024)S(1)}, s32[1024]{0:T(1024)}, u32[]{:S(2)}) copy-start(s32[1024]{0:T(1024)} %param.9) | copy-start | bytes 12292
  158.2 36.3 %all-to-all-start.2 = ((f32[16,32,640]{2,1,0:T(8,128)}), f32[16,32,640]{2,1,0:T(8,128)S(1)}, u32[]{:S(2)}, u32[]{:S(2)}) async-start(f32[16,32,640]{2,1,0:T(8,128)} %broadcast_in_dim.4), calls=%async_computation.2 | async-start | bytes 2621440 | tf_op jit(solution)/shard_map/all_to_all | solution.py:19
  352.3 4.3 %copy-start.1 = (f32[1024,160]{0,1:T(8,128)S(1)}, f32[1024,160]{0,1:T(8,128)}, u32[]{:S(2)}) copy-start(f32[1024,160]{0,1:T(8,128)} %param.7) | copy-start | bytes 1966084
Sparse Core Ops, SparseCore 0:
  9.2 74.9 all-gather.3
  106.2 212.3 all-gather.5
